TPU v7x, 32 devices: a whole 2x2x4 slice. The times are simulated.
32 devices in a mesh: section: 2 (over x), expert: 4 (over y, core), dp: 4 (over z).
Axes of the slice: x: 2, y: 2, z: 4, core: 2. Of those that a mesh axis runs over, the one named last changes fastest.
Arguments:
- tokens: bfloat16 [512, 3072], P('expert', 'dp'), may hold values from -6 to 6
- expert_ids: int32 [512, 2], P('expert'), may hold values from 0 to 3, all different within a row; in each aligned block of 128 rows (0 to 127, 128 to 255, ...) at most 128 rows name the same one
- w_gate: bfloat16 [4, 3072, 8192], P('expert', 'dp', 'section'), may hold values from -0.109375 to 0.109375
- w_up: bfloat16 [4, 3072, 8192], P('expert', 'dp', 'section'), may hold values from -0.109375 to 0.109375
- cotangent: bfloat16 [4, 512, 8192], P('expert', None, 'section'), may hold values from -6 to 6
Outputs:
- acted: bfloat16 [4, 512, 8192], P('expert', None, 'section')
- input_grad: bfloat16 [512, 3072], P('expert', 'dp')
- gate_grad: bfloat16 [4, 3072, 8192], P('expert', 'dp', 'section')
- up_grad: bfloat16 [4, 3072, 8192], P('expert', 'dp', 'section')
Inputs may be any that keep to these rules, and one draw needn't show every extreme that they name: `expert_ids`: each token names two different experts. Among the 128 tokens of one index of the expert axis no expert is named more than 128 times, a bound that some block reaches.
All inputs are finite; a program needn't handle non-finite values.
Results may differ from a plain program's by a relative error of at most 0.0049.
Values may be sent and summed in bfloat16 or wider, within the bound.
No kernel may reach another device: no remote copies, remote signals or barrier semaphores. Data moves between devices by JAX's collectives and lax.ppermute only.
A program may use at most 128 MiB of HBM per device.

v0:
```python
import functools
import math

import jax
import jax.numpy as jnp
from jax import lax
from jax.experimental import pallas as pl
from jax.experimental.pallas import tpu as pltpu
from jax.sharding import PartitionSpec as P

BF, HALF, F32 = jnp.bfloat16, jnp.float16, jnp.float32
BODY, LAG = 256, 3
LIGHT_BODY, LIGHT_LAG = 512, 2
SIDE, MID = [(0, 1), (1, 0), (2, 3), (3, 2)], [(1, 2), (2, 1)]
MIB = 1024 * 1024


def dot(a, b, dims=((1,), (0,))):
    return lax.dot_general(a, b, (dims, ((), ())), preferred_element_type=F32)


def then(value, after):
    return lax.optimization_barrier((value, after))[0]


def swap(value, axis, stride):
    n = lax.axis_size(axis)
    return lax.ppermute(value, axis, [(i, i ^ stride) for i in range(n)])


def gather_expert(value):
    n = lax.axis_size("expert")
    me = lax.axis_index("expert")
    held, stage, stride = value, 0, n // 2
    while stride >= 1:
        other = swap(held, "expert", stride)
        low = (me & stride) == 0
        held = jnp.stack([jnp.where(low, held, other), jnp.where(low, other, held)], axis=stage)
        stage, stride = stage + 1, stride // 2
    return held.reshape((n,) + value.shape)


def scatter_expert(mine, others):
    n = lax.axis_size("expert")
    me = lax.axis_index("expert")
    value = mine + swap(others, "expert", 1).astype(F32)
    stride = 2
    while stride < n:
        value = value.reshape((-1, 2) + value.shape[1:])
        low = (me & stride) == 0
        keep = jnp.where(low, value[:, 0], value[:, 1])
        send = jnp.where(low, value[:, 1], value[:, 0]).astype(BF)
        value = keep + swap(send, "expert", stride).astype(F32)
        stride *= 2
    return value.reshape(value.shape[-2:]).astype(BF)


def chunks_of(total, body):
    body = min(body, total // 2)
    sizes = [body] * (total // body) + ([total % body] if total % body else [])
    return [(sum(sizes[:i]), n) for i, n in enumerate(sizes)]


ANY = pl.BlockSpec(memory_space=pl.ANY)


def whole(shape):
    return pl.BlockSpec(shape, lambda i: (0,) * len(shape))


class Part:
    def __init__(self, at, n):
        self.at, self.n, self.wide = at, n, n if n % 256 else 256
        self.steps = n // self.wide

    def inside(self, height):
        first, steps = self.at // self.wide, self.steps
        return pl.BlockSpec((height, self.wide), lambda i: (0, first + jnp.minimum(i, steps - 1)))

    def own(self, height):
        steps = self.steps
        return pl.BlockSpec((height, 2 * self.wide), lambda i: (0, jnp.minimum(i, steps - 1)))


def call(body, steps, ins, in_specs, outs, out_specs, alias, scratch, vmem):
    return pl.pallas_call(
        body,
        grid=(steps,),
        in_specs=in_specs,
        out_specs=out_specs,
        out_shape=outs,
        scratch_shapes=scratch,
        input_output_aliases=alias,
        compiler_params=pltpu.CompilerParams(vmem_limit_bytes=vmem),
        cost_estimate=pl.CostEstimate(flops=1, bytes_accessed=1, transcendentals=0),
    )(*ins)


def produce_body(x_ref, wg_ref, wu_ref, p_ref):
    n = wg_ref.shape[1]
    p_ref[:, :n] = dot(x_ref[...], wg_ref[...])
    p_ref[:, n:] = dot(x_ref[...], wu_ref[...])


def finish_body(first, packed, x_ref, wg_ref, wu_ref, t_ref, *refs):
    n = wg_ref.shape[1]
    pick_ref = refs[0] if packed else None
    cot_ref, back_in = refs[packed : packed + 2]
    acted_ref, gg_ref, ug_ref, back_ref = refs[-4:]

    @pl.when(first)
    def _():
        back_ref[...] = back_in[...]

    pre_gate, pre_up = t_ref[:, :n], t_ref[:, n:]
    sig = jax.nn.sigmoid(pre_gate)
    silu_v = pre_gate * sig
    cf = dot(pick_ref[...], cot_ref[...]) if packed else cot_ref[...].astype(F32)
    gp = (cf * pre_up * sig * (1.0 + pre_gate * (1.0 - sig))).astype(BF)
    up = (cf * silu_v).astype(BF)
    acted = (silu_v * pre_up).astype(BF)
    acted_ref[...] = dot(pick_ref[...], acted, ((0,), (0,))).astype(BF) if packed else acted
    gg_ref[...] = dot(x_ref[...], gp, ((0,), (0,))).astype(BF)
    ug_ref[...] = dot(x_ref[...], up, ((0,), (0,))).astype(BF)
    back_ref[...] += dot(gp, wg_ref[...], ((1,), (1,))) + dot(up, wu_ref[...], ((1,), (1,)))


def main_call(x, wg, wu, make=None, end=None):
    rows, width = x.shape
    ins, in_specs = [x], [whole(x.shape)]
    outs, out_specs, alias, scratch = [], [], {}, []
    end_steps = make_steps = 0
    if end is not None:
        part, t, pick, cot, acted, gg, ug, back = end
        packed = int(pick is not None)
        end_steps = part.steps
        for arr, spec, into in (
            (wg, part.inside(width), None),
            (wu, part.inside(width), None),
            (t, part.own(rows), None),
            (pick, None if pick is None else whole(pick.shape), None),
            (cot, part.inside(cot.shape[0]), None),
            (back, whole(back.shape), 3),
            (acted, ANY, 0),
            (gg, ANY, 1),
            (ug, ANY, 2),
        ):
            if arr is None:
                continue
            if into is not None:
                alias[len(ins)] = into
            ins.append(arr)
            in_specs.append(spec)
        outs += [jax.ShapeDtypeStruct(v, BF) for v in (cot.shape, wg.shape, wg.shape)]
        outs += [jax.ShapeDtypeStruct(back.shape, F32)]
        out_specs += [part.inside(cot.shape[0]), part.inside(width), part.inside(width), whole(back.shape)]
    if make is not None:
        make, full = make
        make_steps = make.steps
        ins += [wg, wu]
        in_specs += [make.inside(width)] * 2
        outs.append(jax.ShapeDtypeStruct((rows, full), F32))
        out_specs.append(make.own(rows))
    n_in = len(ins)

    def body(*refs):
        i, o = refs[:n_in], refs[n_in:]
        step = pl.program_id(0)
        if make is not None:

            @pl.when(step < make_steps)
            def _():
                produce_body(i[0], i[-2], i[-1], o[-1])

        if end is not None:

            @pl.when(step < end_steps)
            def _():
                finish_body(step == 0, packed, *i[: 6 + packed], *o[:4])

    return call(body, max(end_steps, make_steps), ins, in_specs, outs, out_specs, alias, scratch, 30 * MIB)


def pipeline(rows, cap, scale, tokens, hit, rank, wg, wu, cot):
    groups, per = hit.shape
    width, hidden = wg.shape
    count = jnp.sum(hit.astype(F32), axis=1)
    packed = rows < groups * cap
    first = jnp.cumsum(count) - count if packed else cap * jnp.arange(groups, dtype=F32)
    place = jnp.where(hit, first[:, None] + rank, -1.0).reshape(1, groups * per)
    row = jnp.arange(rows, dtype=F32)[:, None]
    take = (row == place).astype(BF)
    x = dot(take, tokens).astype(BF)
    pick = None
    if packed:
        slot = jnp.arange(cap, dtype=F32)[None, :]
        slot_row = jnp.where(slot < count[:, None], first[:, None] + slot, -1.0).reshape(1, groups * cap)
        pick = (row == slot_row).astype(BF)

    dp = lax.axis_index("dp")
    inner = (dp == 1) | (dp == 2)
    body, lag = (BODY, LAG) if 2 * rows > groups * cap else (LIGHT_BODY, LIGHT_LAG)
    parts = [Part(at, n) for at, n in chunks_of(hidden, body)]
    full = 2 * parts[0].n
    acted = gg = ug = None
    back = jnp.zeros((rows, width), F32)
    token = x
    p, q, b, sent, got = {}, {}, {}, {}, {}
    last = len(parts)
    lag = min(lag, last)

    def finish(j):
        nonlocal token, acted, gg, ug, back
        both = jnp.where(inner, sent.pop(j + lag), got.pop(j + lag)).astype(F32) * (1.0 / scale)
        args = (parts[j], both, pick, cot, acted, gg, ug, back)
        acted, gg, ug, back = main_call(then(x, token), wg, wu, None, args)
        token = back

    def make(j):
        p[j] = (main_call(then(x, token), wg, wu, (parts[j], full))[0] * scale).astype(HALF)

    def add(one, two):
        return (one.astype(F32) + two.astype(F32)).astype(HALF)

    def side(j):
        nonlocal token
        i = j - lag
        if i >= 0:
            total = add(q.pop(i), then(b.pop(i), token))
            sent[j] = token = jnp.where(inner, total, p[j]) if j < last else total
        else:
            sent[j] = then(p[j], token)
        got[j] = lax.ppermute(sent[j], "dp", SIDE)

    for j in range(min(lag - 1, last)):
        make(j)
        side(j)
    for j in range(lag - 1, min(4, last)):
        make(j)
    for k in range(last + lag):
        if k < last:
            q[k] = token = add(p.pop(k), then(got[k], token))
            b[k] = lax.ppermute(q[k], "dp", MID)
        if k + lag - 1 < last + lag:
            side(k + lag - 1)
        for j in (2 * k + 4, 2 * k + 5):
            if j < last:
                make(j)
        if k >= lag:
            finish(k - lag)
    by_bit = take.reshape(rows, -1, 2, per)
    bit = lax.axis_index("expert") & 1
    low = back.astype(BF)
    mine, others = [
        dot(lax.dynamic_index_in_dim(by_bit, which, 2, False).reshape(rows, -1), low, ((0,), (0,)))
        for which in (bit, 1 - bit)
    ]
    return acted, gg, ug, mine, others.astype(BF)


def local(tokens, expert_ids, w_gate, w_up, cotangent):
    rows, width = tokens.shape
    experts = lax.axis_size("expert")
    cap = min(rows, 4 * rows // experts)
    wg, wu, cot = w_gate[0], w_up[0], cotangent[0]
    me = lax.axis_index("expert")
    bound = 6.0 * 0.109375 * width * lax.axis_size("dp")
    scale = 2.0 ** math.floor(math.log2(65000.0 / bound))
    ids = jnp.pad(expert_ids.astype(BF), ((0, 0), (0, 126)))
    held = gather_expert(jnp.concatenate([tokens, ids], axis=1))
    all_tokens, all_ids = held[:, :, :width], held[:, :, width : width + 2]
    hit = jnp.any(all_ids == me.astype(BF), axis=2)
    before = (jnp.arange(rows)[:, None] < jnp.arange(rows)[None, :]).astype(BF)
    rank = dot(hit.astype(BF), before)
    slots = experts * cap
    sizes = sorted({slots * part // 16 for part in (6, 8, 16)}, reverse=True)
    filled = jnp.sum(hit.astype(jnp.int32))
    which = jnp.sum((filled <= jnp.array(sizes[1:], jnp.int32)).astype(jnp.int32))
    acted, gg, ug, mine, others = lax.switch(
        which,
        [functools.partial(pipeline, size, cap, scale) for size in sizes],
        all_tokens.reshape(experts * rows, width),
        hit,
        rank,
        wg,
        wu,
        cot,
    )
    halves = (experts // 2, rows, width)
    part = scatter_expert(mine.reshape(halves), others.reshape(halves))
    if lax.axis_size("section") == 2:
        total = part.astype(F32) + swap(part, "section", 1).astype(F32)
    else:
        total = lax.psum(part.astype(F32), "section")
    return acted[None], total.astype(BF), gg[None], ug[None]


def solution(mesh):
    placed = (
        P("expert", "dp"),
        P("expert", None),
        P("expert", "dp", "section"),
        P("expert", "dp", "section"),
        P("expert", None, "section"),
    )
    return jax.shard_map(
        local,
        mesh=mesh,
        in_specs=placed,
        out_specs=(
            P("expert", None, "section"),
            P("expert", "dp"),
            P("expert", "dp", "section"),
            P("expert", "dp", "section"),
        ),
        check_vma=False,
    )
```

profile of v0, /device:TPU:0, one launch (start us, length us, event | category | flops | bytes accessed | tf_op | source)
XLA Modules:
  0.0 222.7 jit_solution(6705961569276519220)
XLA Ops:
  5.5 5.6 %collective-permute-done.71 = bf16[128,896]{1,0:T(8,128)(2,1)S(1)} collective-permute-done((bf16[128,896]{1,0:T(8,128)(2,1)S(1)}, bf16[128,896]{1,0:T(8,128)(2,1)S(1)}, u32[]{:S(2)}, u32[]{:S(2)}) %collective-permute-start.71) | collective-permute-done | bytes 229408 | tf_op jit(solution)/shard_map/ppermute | solution.py:28
  17.1 146.0 %conditional.2 = (bf16[512,4096]{1,0:T(8,128)(2,1)}, bf16[768,4096]{1,0:T(8,128)(2,1)}, bf16[768,4096]{1,0:T(8,128)(2,1)}, bf16[256,768]{1,0:T(8,128)(2,1)S(1)}, f32[2,128,768]{2,1,0:T(8,128)S(1)}) conditional(s32[]{:T(128)} %clamp.3, (f32[4,128]{1,0:T(4,128)S(1)}, pred[4,128]{1,0:T(4,128)(4,1)S(1)}, ...), branch_computations={%region_3.4_spmd, %region_4.7_spmd, %region_7.10_spmd} | conditional | flops 873333760 | bytes 297162880
  47.1 7.5 %collective-permute-done.53 = f16[192,1024]{1,0:T(8,128)(2,1)S(1)} collective-permute-done((f16[192,1024]{1,0:T(8,128)(2,1)S(1)}, f16[192,1024]{1,0:T(8,128)(2,1)S(1)}, u32[]{:S(2)}, u32[]{:S(2)}) %collective-permute-start.53) | collective-permute-done | bytes 393248 | tf_op jit(solution)/shard_map/cond/branch_2_fun/ppermute | solution.py:233
  58.2 6.9 %collective-permute-done.55 = f16[192,1024]{1,0:T(8,128)(2,1)S(1)} collective-permute-done((f16[192,1024]{1,0:T(8,128)(2,1)S(1)}, f16[192,1024]{1,0:T(8,128)(2,1)S(1)}, u32[]{:S(2)}, u32[]{:S(2)}) %collective-permute-start.55) | collective-permute-done | bytes 393248 | tf_op jit(solution)/shard_map/cond/branch_2_fun/ppermute | solution.py:233
  65.6 4.6 %collective-permute-start.57 = (f16[192,1024]{1,0:T(8,128)(2,1)S(1)}, f16[192,1024]{1,0:T(8,128)(2,1)S(1)}, u32[]{:S(2)}, u32[]{:S(2)}) collective-permute-start(f16[192,1024]{1,0:T(8,128)(2,1)S(1)} %fusion.38), channel_id=1, source_target_pairs={{0,1},{1,0},{2,3},{3,2},{4,5},{5,4},{6,7},{7,6},{8,9},{9,8},{10,11... | collective-permute-start | bytes 1179656 | tf_op jit(solution)/shard_map/cond/branch_2_fun/ppermute | solution.py:233
  72.8 5.1 %collective-permute-done.57 = f16[192,1024]{1,0:T(8,128)(2,1)S(1)} collective-permute-done((f16[192,1024]{1,0:T(8,128)(2,1)S(1)}, f16[192,1024]{1,0:T(8,128)(2,1)S(1)}, u32[]{:S(2)}, u32[]{:S(2)}) %collective-permute-start.57) | collective-permute-done | bytes 393248 | tf_op jit(solution)/shard_map/cond/branch_2_fun/ppermute | solution.py:233
  78.2 4.0 %collective-permute-start.58 = (f16[192,1024]{1,0:T(8,128)(2,1)S(1)}, f16[192,1024]{1,0:T(8,128)(2,1)S(1)}, u32[]{:S(2)}, u32[]{:S(2)}) collective-permute-start(f16[192,1024]{1,0:T(8,128)(2,1)S(1)} %fusion.39), channel_id=1, source_target_pairs={{0,1},{1,0},{2,3},{3,2},{4,5},{5,4},{6,7},{7,6},{8,9},{9,8},{10,11... | collective-permute-start | bytes 1179656 | tf_op jit(solution)/shard_map/cond/branch_2_fun/ppermute | solution.py:233
  89.3 4.8 %collective-permute-start.61 = (f16[192,1024]{1,0:T(8,128)(2,1)S(1)}, f16[192,1024]{1,0:T(8,128)(2,1)S(1)}, u32[]{:S(2)}, u32[]{:S(2)}) collective-permute-start(f16[192,1024]{1,0:T(8,128)(2,1)S(1)} %fusion.40), channel_id=1, source_target_pairs={{0,1},{1,0},{2,3},{3,2},{4,5},{5,4},{6,7},{7,6},{8,9},{9,8},{10,11... | collective-permute-start | bytes 1179656 | tf_op jit(solution)/shard_map/cond/branch_2_fun/ppermute | solution.py:233
  95.9 3.2 %branch_2_fun.24 = (bf16[512,4096]{1,0:T(8,128)(2,1)}, bf16[768,4096]{1,0:T(8,128)(2,1)}, bf16[768,4096]{1,0:T(8,128)(2,1)}, f32[192,768]{1,0:T(8,128)S(1)}) custom-call(bf16[192,768]{1,0:T(8,128)(2,1)S(1)} %convolution_convert_fusion.2.refs_0_, ...), custom_call_target="tpu_custom_call", output_to_operand_aliasing={{3}: (6, {}), {0}: (7, {}), {1}: (8, {}), {2}: (9, {})} | custom-call | flops 1 | bytes 1 | tf_op jit(solution)/shard_map/cond/branch_2_fun/pallas_call | solution.py:86
  100.3 4.8 %collective-permute-start.62 = (f16[192,1024]{1,0:T(8,128)(2,1)S(1)}, f16[192,1024]{1,0:T(8,128)(2,1)S(1)}, u32[]{:S(2)}, u32[]{:S(2)}) collective-permute-start(f16[192,1024]{1,0:T(8,128)(2,1)S(1)} %fusion.41), channel_id=1, source_target_pairs={{0,1},{1,0},{2,3},{3,2},{4,5},{5,4},{6,7},{7,6},{8,9},{9,8},{10,11... | collective-permute-start | bytes 1179656 | tf_op jit(solution)/shard_map/cond/branch_2_fun/ppermute | solution.py:233
  106.9 3.2 %branch_2_fun.25 = (bf16[512,4096]{1,0:T(8,128)(2,1)}, bf16[768,4096]{1,0:T(8,128)(2,1)}, bf16[768,4096]{1,0:T(8,128)(2,1)}, f32[192,768]{1,0:T(8,128)S(1)}) custom-call(bf16[192,768]{1,0:T(8,128)(2,1)S(1)} %convolution_convert_fusion.2.refs_0_, ...), custom_call_target="tpu_custom_call", output_to_operand_aliasing={{3}: (6, {}), {0}: (7, {}), {1}: (8, {}), {2}: (9, {})} | custom-call | flops 1 | bytes 1 | tf_op jit(solution)/shard_map/cond/branch_2_fun/pallas_call | solution.py:86
  111.2 4.9 %collective-permute-start.65 = (f16[192,1024]{1,0:T(8,128)(2,1)S(1)}, f16[192,1024]{1,0:T(8,128)(2,1)S(1)}, u32[]{:S(2)}, u32[]{:S(2)}) collective-permute-start(f16[192,1024]{1,0:T(8,128)(2,1)S(1)} %fusion.42), channel_id=1, source_target_pairs={{0,1},{1,0},{2,3},{3,2},{4,5},{5,4},{6,7},{7,6},{8,9},{9,8},{10,11... | collective-permute-start | bytes 1179656 | tf_op jit(solution)/shard_map/cond/branch_2_fun/ppermute | solution.py:233
  117.9 3.2 %branch_2_fun.27 = (bf16[512,4096]{1,0:T(8,128)(2,1)}, bf16[768,4096]{1,0:T(8,128)(2,1)}, bf16[768,4096]{1,0:T(8,128)(2,1)}, f32[192,768]{1,0:T(8,128)S(1)}) custom-call(bf16[192,768]{1,0:T(8,128)(2,1)S(1)} %convolution_convert_fusion.2.refs_0_, ...), custom_call_target="tpu_custom_call", output_to_operand_aliasing={{3}: (6, {}), {0}: (7, {}), {1}: (8, {}), {2}: (9, {})} | custom-call | flops 1 | bytes 1 | tf_op jit(solution)/shard_map/cond/branch_2_fun/pallas_call | solution.py:86
  122.1 6.0 %collective-permute-start.66 = (f16[192,1024]{1,0:T(8,128)(2,1)S(1)}, f16[192,1024]{1,0:T(8,128)(2,1)S(1)}, u32[]{:S(2)}, u32[]{:S(2)}) collective-permute-start(f16[192,1024]{1,0:T(8,128)(2,1)S(1)} %fusion.43), channel_id=1, source_target_pairs={{0,1},{1,0},{2,3},{3,2},{4,5},{5,4},{6,7},{7,6},{8,9},{9,8},{10,11... | collective-permute-start | bytes 1179656 | tf_op jit(solution)/shard_map/cond/branch_2_fun/ppermute | solution.py:233
  129.3 3.2 %branch_2_fun.28 = (bf16[512,4096]{1,0:T(8,128)(2,1)}, bf16[768,4096]{1,0:T(8,128)(2,1)}, bf16[768,4096]{1,0:T(8,128)(2,1)}, f32[192,768]{1,0:T(8,128)S(1)}) custom-call(bf16[192,768]{1,0:T(8,128)(2,1)S(1)} %convolution_convert_fusion.2.refs_0_, ...), custom_call_target="tpu_custom_call", output_to_operand_aliasing={{3}: (6, {}), {0}: (7, {}), {1}: (8, {}), {2}: (9, {})} | custom-call | flops 1 | bytes 1 | tf_op jit(solution)/shard_map/cond/branch_2_fun/pallas_call | solution.py:86
  132.5 3.2 %collective-permute-done.66 = f16[192,1024]{1,0:T(8,128)(2,1)S(1)} collective-permute-done((f16[192,1024]{1,0:T(8,128)(2,1)S(1)}, f16[192,1024]{1,0:T(8,128)(2,1)S(1)}, u32[]{:S(2)}, u32[]{:S(2)}) %collective-permute-start.66) | collective-permute-done | bytes 393248 | tf_op jit(solution)/shard_map/cond/branch_2_fun/ppermute | solution.py:233
  136.6 5.7 %collective-permute-start.69 = (f16[192,1024]{1,0:T(8,128)(2,1)S(1)}, f16[192,1024]{1,0:T(8,128)(2,1)S(1)}, u32[]{:S(2)}, u32[]{:S(2)}) collective-permute-start(f16[192,1024]{1,0:T(8,128)(2,1)S(1)} %add_convert_fusion.49), channel_id=1, source_target_pairs={{0,1},{1,0},{2,3},{3,2},{4,5},{5,4},{6,7},{7,6},{8,9},{9,8},{10,11... | collective-permute-start | bytes 1179656 | tf_op jit(solution)/shard_map/cond/branch_2_fun/ppermute | solution.py:233
  142.4 3.2 %branch_2_fun.29 = (bf16[512,4096]{1,0:T(8,128)(2,1)}, bf16[768,4096]{1,0:T(8,128)(2,1)}, bf16[768,4096]{1,0:T(8,128)(2,1)}, f32[192,768]{1,0:T(8,128)S(1)}) custom-call(bf16[192,768]{1,0:T(8,128)(2,1)S(1)} %convolution_convert_fusion.2.refs_0_, ...), custom_call_target="tpu_custom_call", output_to_operand_aliasing={{3}: (6, {}), {0}: (7, {}), {1}: (8, {}), {2}: (9, {})} | custom-call | flops 1 | bytes 1 | tf_op jit(solution)/shard_map/cond/branch_2_fun/pallas_call | solution.py:86
  149.7 4.2 %collective-permute-done.70 = f16[192,1024]{1,0:T(8,128)(2,1)S(1)} collective-permute-done((f16[192,1024]{1,0:T(8,128)(2,1)S(1)}, f16[192,1024]{1,0:T(8,128)(2,1)S(1)}, u32[]{:S(2)}, u32[]{:S(2)}) %collective-permute-start.70) | collective-permute-done | bytes 393248 | tf_op jit(solution)/shard_map/cond/branch_2_fun/ppermute | solution.py:233
  154.2 4.2 %branch_2_fun.30 = (bf16[512,4096]{1,0:T(8,128)(2,1)}, bf16[768,4096]{1,0:T(8,128)(2,1)}, bf16[768,4096]{1,0:T(8,128)(2,1)}, f32[192,768]{1,0:T(8,128)S(1)}) custom-call(bf16[192,768]{1,0:T(8,128)(2,1)S(1)} %convolution_convert_fusion.2.refs_0_, ...), custom_call_target="tpu_custom_call", output_to_operand_aliasing={{3}: (6, {}), {0}: (7, {}), {1}: (8, {}), {2}: (9, {})} | custom-call | flops 1 | bytes 1 | tf_op jit(solution)/shard_map/cond/branch_2_fun/pallas_call | solution.py:86
  158.4 3.9 %branch_2_fun.31 = (bf16[512,4096]{1,0:T(8,128)(2,1)}, bf16[768,4096]{1,0:T(8,128)(2,1)}, bf16[768,4096]{1,0:T(8,128)(2,1)}, f32[192,768]{1,0:T(8,128)S(1)}) custom-call(bf16[192,768]{1,0:T(8,128)(2,1)S(1)} %convolution_convert_fusion.2.refs_0_, ...), custom_call_target="tpu_custom_call", output_to_operand_aliasing={{3}: (6, {}), {0}: (7, {}), {1}: (8, {}), {2}: (9, {})} | custom-call | flops 1 | bytes 1 | tf_op jit(solution)/shard_map/cond/branch_2_fun/pallas_call | solution.py:86
  165.0 44.7 %collective-permute-start.74 = (bf16[1,128,768]{2,1,0:T(8,128)(2,1)S(1)}, bf16[1,128,768]{2,1,0:T(8,128)(2,1)S(1)}, u32[]{:S(2)}, u32[]{:S(2)}) collective-permute-start(bf16[1,128,768]{2,1,0:T(8,128)(2,1)S(1)} %fusion.57), channel_id=1, source_target_pairs={{0,8},{4,12},{8,0},{12,4},{1,9},{5,13},{9,1},{13,5},{2,10},{6,14},... | collective-permute-start | bytes 589832 | tf_op jit(solution)/shard_map/ppermute | solution.py:28
  209.7 5.2 %collective-permute-done.74 = bf16[1,128,768]{2,1,0:T(8,128)(2,1)S(1)} collective-permute-done((bf16[1,128,768]{2,1,0:T(8,128)(2,1)S(1)}, bf16[1,128,768]{2,1,0:T(8,128)(2,1)S(1)}, u32[]{:S(2)}, u32[]{:S(2)}) %collective-permute-start.74) | collective-permute-done | bytes 196640 | tf_op jit(solution)/shard_map/ppermute | solution.py:28
  216.6 4.9 %collective-permute-done.75 = bf16[128,768]{1,0:T(8,128)(2,1)S(1)} collective-permute-done((bf16[128,768]{1,0:T(8,128)(2,1)S(1)}, bf16[128,768]{1,0:T(8,128)(2,1)S(1)}, u32[]{:S(2)}, u32[]{:S(2)}) %collective-permute-start.75) | collective-permute-done | bytes 196640 | tf_op jit(solution)/shard_map/ppermute | solution.py:28
  (115 shorter events, 50.6 us)
Async XLA Ops:
  2.4 8.6 %collective-permute-start.71 = (bf16[128,896]{1,0:T(8,128)(2,1)S(1)}, bf16[128,896]{1,0:T(8,128)(2,1)S(1)}, u32[]{:S(2)}, u32[]{:S(2)}) collective-permute-start(bf16[128,896]{1,0:T(8,128)(2,1)S(1)} %fusion.56), channel_id=1, source_target_pairs={{0,8},{4,12},{8,0},{12,4},{1,9},{5,13},{9,1},{13,5},{2,10},{6,14},... | collective-permute-start | bytes 688136 | tf_op jit(solution)/shard_map/ppermute | solution.py:28
  12.1 1.9 collective-permute-start.72
  43.3 11.3 %collective-permute-start.53 = (f16[192,1024]{1,0:T(8,128)(2,1)S(1)}, f16[192,1024]{1,0:T(8,128)(2,1)S(1)}, u32[]{:S(2)}, u32[]{:S(2)}) collective-permute-start(f16[192,1024]{1,0:T(8,128)(2,1)S(1)} %multiply_convert_fusion.31), channel_id=1, source_target_pairs={{0,1},{1,0},{2,3},{3,2},{4,5},{5,4},{6,7},{7,6},{8,9},{9,8},{10,11... | collective-permute-start | bytes 1179656 | tf_op jit(solution)/shard_map/cond/branch_2_fun/ppermute | solution.py:233
  54.7 10.5 %collective-permute-start.55 = (f16[192,1024]{1,0:T(8,128)(2,1)S(1)}, f16[192,1024]{1,0:T(8,128)(2,1)S(1)}, u32[]{:S(2)}, u32[]{:S(2)}) collective-permute-start(f16[192,1024]{1,0:T(8,128)(2,1)S(1)} %multiply_convert_fusion.30), channel_id=1, source_target_pairs={{0,1},{1,0},{2,3},{3,2},{4,5},{5,4},{6,7},{7,6},{8,9},{9,8},{10,11... | collective-permute-start | bytes 1179656 | tf_op jit(solution)/shard_map/cond/branch_2_fun/ppermute | solution.py:233
  56.5 8.8 %collective-permute-start.54 = (f16[192,1024]{1,0:T(8,128)(2,1)S(1)}, f16[192,1024]{1,0:T(8,128)(2,1)S(1)}, u32[]{:S(2)}, u32[]{:S(2)}) collective-permute-start(f16[192,1024]{1,0:T(8,128)(2,1)S(1)} %add_convert_fusion.63), channel_id=1, source_target_pairs={{1,2},{2,1},{5,6},{6,5},{9,10},{10,9},{13,14},{14,13},{17,18},{18,... | collective-permute-start | bytes 1179656 | tf_op jit(solution)/shard_map/cond/branch_2_fun/ppermute | solution.py:243
  65.3 16.9 %slice-start.12 = ((s8[6291456]{0:T(1024)(128)(4,1)}), s8[4194304]{0:T(1024)(128)(4,1)S(1)}, s32[]{:S(2)}) async-start(s8[6291456]{0:T(1024)(128)(4,1)} %bitcast.102), calls=%async_computation.12 | async-start | bytes 8388608 | tf_op jit(solution)/shard_map/conditional
  65.6 12.3 %collective-permute-start.57 = (f16[192,1024]{1,0:T(8,128)(2,1)S(1)}, f16[192,1024]{1,0:T(8,128)(2,1)S(1)}, u32[]{:S(2)}, u32[]{:S(2)}) collective-permute-start(f16[192,1024]{1,0:T(8,128)(2,1)S(1)} %fusion.38), channel_id=1, source_target_pairs={{0,1},{1,0},{2,3},{3,2},{4,5},{5,4},{6,7},{7,6},{8,9},{9,8},{10,11... | collective-permute-start | bytes 1179656 | tf_op jit(solution)/shard_map/cond/branch_2_fun/ppermute | solution.py:233
  70.2 7.8 %collective-permute-start.56 = (f16[192,1024]{1,0:T(8,128)(2,1)S(1)}, f16[192,1024]{1,0:T(8,128)(2,1)S(1)}, u32[]{:S(2)}, u32[]{:S(2)}) collective-permute-start(f16[192,1024]{1,0:T(8,128)(2,1)S(1)} %add_convert_fusion.62), channel_id=1, source_target_pairs={{1,2},{2,1},{5,6},{6,5},{9,10},{10,9},{13,14},{14,13},{17,18},{18,... | collective-permute-start | bytes 1179656 | tf_op jit(solution)/shard_map/cond/branch_2_fun/ppermute | solution.py:243
  78.2 10.7 %collective-permute-start.58 = (f16[192,1024]{1,0:T(8,128)(2,1)S(1)}, f16[192,1024]{1,0:T(8,128)(2,1)S(1)}, u32[]{:S(2)}, u32[]{:S(2)}) collective-permute-start(f16[192,1024]{1,0:T(8,128)(2,1)S(1)} %fusion.39), channel_id=1, source_target_pairs={{0,1},{1,0},{2,3},{3,2},{4,5},{5,4},{6,7},{7,6},{8,9},{9,8},{10,11... | collective-permute-start | bytes 1179656 | tf_op jit(solution)/shard_map/cond/branch_2_fun/ppermute | solution.py:233
  83.3 5.7 %collective-permute-start.60 = (f16[192,1024]{1,0:T(8,128)(2,1)S(1)}, f16[192,1024]{1,0:T(8,128)(2,1)S(1)}, u32[]{:S(2)}, u32[]{:S(2)}) collective-permute-start(f16[192,1024]{1,0:T(8,128)(2,1)S(1)} %add_convert_fusion.60), channel_id=1, source_target_pairs={{1,2},{2,1},{5,6},{6,5},{9,10},{10,9},{13,14},{14,13},{17,18},{18,... | collective-permute-start | bytes 1179656 | tf_op jit(solution)/shard_map/cond/branch_2_fun/ppermute | solution.py:243
  89.3 10.7 %collective-permute-start.61 = (f16[192,1024]{1,0:T(8,128)(2,1)S(1)}, f16[192,1024]{1,0:T(8,128)(2,1)S(1)}, u32[]{:S(2)}, u32[]{:S(2)}) collective-permute-start(f16[192,1024]{1,0:T(8,128)(2,1)S(1)} %fusion.40), channel_id=1, source_target_pairs={{0,1},{1,0},{2,3},{3,2},{4,5},{5,4},{6,7},{7,6},{8,9},{9,8},{10,11... | collective-permute-start | bytes 1179656 | tf_op jit(solution)/shard_map/cond/branch_2_fun/ppermute | solution.py:233
  95.1 5.0 %collective-permute-start.59 = (f16[192,1024]{1,0:T(8,128)(2,1)S(1)}, f16[192,1024]{1,0:T(8,128)(2,1)S(1)}, u32[]{:S(2)}, u32[]{:S(2)}) collective-permute-start(f16[192,1024]{1,0:T(8,128)(2,1)S(1)} %add_convert_fusion.58), channel_id=1, source_target_pairs={{1,2},{2,1},{5,6},{6,5},{9,10},{10,9},{13,14},{14,13},{17,18},{18,... | collective-permute-start | bytes 1179656 | tf_op jit(solution)/shard_map/cond/branch_2_fun/ppermute | solution.py:243
  100.3 10.6 %collective-permute-start.62 = (f16[192,1024]{1,0:T(8,128)(2,1)S(1)}, f16[192,1024]{1,0:T(8,128)(2,1)S(1)}, u32[]{:S(2)}, u32[]{:S(2)}) collective-permute-start(f16[192,1024]{1,0:T(8,128)(2,1)S(1)} %fusion.41), channel_id=1, source_target_pairs={{0,1},{1,0},{2,3},{3,2},{4,5},{5,4},{6,7},{7,6},{8,9},{9,8},{10,11... | collective-permute-start | bytes 1179656 | tf_op jit(solution)/shard_map/cond/branch_2_fun/ppermute | solution.py:233
  106.1 4.9 %collective-permute-start.64 = (f16[192,1024]{1,0:T(8,128)(2,1)S(1)}, f16[192,1024]{1,0:T(8,128)(2,1)S(1)}, u32[]{:S(2)}, u32[]{:S(2)}) collective-permute-start(f16[192,1024]{1,0:T(8,128)(2,1)S(1)} %add_convert_fusion.56), channel_id=1, source_target_pairs={{1,2},{2,1},{5,6},{6,5},{9,10},{10,9},{13,14},{14,13},{17,18},{18,... | collective-permute-start | bytes 1179656 | tf_op jit(solution)/shard_map/cond/branch_2_fun/ppermute | solution.py:243
  111.2 10.6 %collective-permute-start.65 = (f16[192,1024]{1,0:T(8,128)(2,1)S(1)}, f16[192,1024]{1,0:T(8,128)(2,1)S(1)}, u32[]{:S(2)}, u32[]{:S(2)}) collective-permute-start(f16[192,1024]{1,0:T(8,128)(2,1)S(1)} %fusion.42), channel_id=1, source_target_pairs={{0,1},{1,0},{2,3},{3,2},{4,5},{5,4},{6,7},{7,6},{8,9},{9,8},{10,11... | collective-permute-start | bytes 1179656 | tf_op jit(solution)/shard_map/cond/branch_2_fun/ppermute | solution.py:233
  117.0 4.9 %collective-permute-start.63 = (f16[192,1024]{1,0:T(8,128)(2,1)S(1)}, f16[192,1024]{1,0:T(8,128)(2,1)S(1)}, u32[]{:S(2)}, u32[]{:S(2)}) collective-permute-start(f16[192,1024]{1,0:T(8,128)(2,1)S(1)} %add_convert_fusion.54), channel_id=1, source_target_pairs={{1,2},{2,1},{5,6},{6,5},{9,10},{10,9},{13,14},{14,13},{17,18},{18,... | collective-permute-start | bytes 1179656 | tf_op jit(solution)/shard_map/cond/branch_2_fun/ppermute | solution.py:243
  122.1 13.5 %collective-permute-start.66 = (f16[192,1024]{1,0:T(8,128)(2,1)S(1)}, f16[192,1024]{1,0:T(8,128)(2,1)S(1)}, u32[]{:S(2)}, u32[]{:S(2)}) collective-permute-start(f16[192,1024]{1,0:T(8,128)(2,1)S(1)} %fusion.43), channel_id=1, source_target_pairs={{0,1},{1,0},{2,3},{3,2},{4,5},{5,4},{6,7},{7,6},{8,9},{9,8},{10,11... | collective-permute-start | bytes 1179656 | tf_op jit(solution)/shard_map/cond/branch_2_fun/ppermute | solution.py:233
  128.2 8.3 %collective-permute-start.68 = (f16[192,1024]{1,0:T(8,128)(2,1)S(1)}, f16[192,1024]{1,0:T(8,128)(2,1)S(1)}, u32[]{:S(2)}, u32[]{:S(2)}) collective-permute-start(f16[192,1024]{1,0:T(8,128)(2,1)S(1)} %add_convert_fusion.52), channel_id=1, source_target_pairs={{1,2},{2,1},{5,6},{6,5},{9,10},{10,9},{13,14},{14,13},{17,18},{18,... | collective-permute-start | bytes 1179656 | tf_op jit(solution)/shard_map/cond/branch_2_fun/ppermute | solution.py:243
  135.8 9.8 %collective-permute-start.67 = (f16[192,1024]{1,0:T(8,128)(2,1)S(1)}, f16[192,1024]{1,0:T(8,128)(2,1)S(1)}, u32[]{:S(2)}, u32[]{:S(2)}) collective-permute-start(f16[192,1024]{1,0:T(8,128)(2,1)S(1)} %add_convert_fusion.50), channel_id=1, source_target_pairs={{1,2},{2,1},{5,6},{6,5},{9,10},{10,9},{13,14},{14,13},{17,18},{18,... | collective-permute-start | bytes 1179656 | tf_op jit(solution)/shard_map/cond/branch_2_fun/ppermute | solution.py:243
  136.6 13.0 %collective-permute-start.69 = (f16[192,1024]{1,0:T(8,128)(2,1)S(1)}, f16[192,1024]{1,0:T(8,128)(2,1)S(1)}, u32[]{:S(2)}, u32[]{:S(2)}) collective-permute-start(f16[192,1024]{1,0:T(8,128)(2,1)S(1)} %add_convert_fusion.49), channel_id=1, source_target_pairs={{0,1},{1,0},{2,3},{3,2},{4,5},{5,4},{6,7},{7,6},{8,9},{9,8},{10,11... | collective-permute-start | bytes 1179656 | tf_op jit(solution)/shard_map/cond/branch_2_fun/ppermute | solution.py:233
  145.8 8.1 %collective-permute-start.70 = (f16[192,1024]{1,0:T(8,128)(2,1)S(1)}, f16[192,1024]{1,0:T(8,128)(2,1)S(1)}, u32[]{:S(2)}, u32[]{:S(2)}) collective-permute-start(f16[192,1024]{1,0:T(8,128)(2,1)S(1)} %add_convert_fusion.48), channel_id=1, source_target_pairs={{0,1},{1,0},{2,3},{3,2},{4,5},{5,4},{6,7},{7,6},{8,9},{9,8},{10,11... | collective-permute-start | bytes 1179656 | tf_op jit(solution)/shard_map/cond/branch_2_fun/ppermute | solution.py:233
  163.1 1.8 collective-permute-start.73
  165.0 49.9 %collective-permute-start.74 = (bf16[1,128,768]{2,1,0:T(8,128)(2,1)S(1)}, bf16[1,128,768]{2,1,0:T(8,128)(2,1)S(1)}, u32[]{:S(2)}, u32[]{:S(2)}) collective-permute-start(bf16[1,128,768]{2,1,0:T(8,128)(2,1)S(1)} %fusion.57), channel_id=1, source_target_pairs={{0,8},{4,12},{8,0},{12,4},{1,9},{5,13},{9,1},{13,5},{2,10},{6,14},... | collective-permute-start | bytes 589832 | tf_op jit(solution)/shard_map/ppermute | solution.py:28
  215.0 6.5 %collective-permute-start.75 = (bf16[128,768]{1,0:T(8,128)(2,1)S(1)}, bf16[128,768]{1,0:T(8,128)(2,1)S(1)}, u32[]{:S(2)}, u32[]{:S(2)}) collective-permute-start(bf16[128,768]{1,0:T(8,128)(2,1)S(1)} %fusion.58), channel_id=1, source_target_pairs={{0,16},{16,0},{1,17},{17,1},{2,18},{18,2},{3,19},{19,3},{4,20},{20... | collective-permute-start | bytes 589832 | tf_op jit(solution)/shard_map/ppermute | solution.py:28
  (9 other events, 84.5 us)
where the time goes:
time: 226 us; the launch traced here: 223 us
  starting transfers between devices  95.9 us (42%)
  waiting for transfers between devices  51.1 us (23%)
  Pallas kernels  37.2 us (16%)
  loops' own time  24.1 us (11%)
  other arithmetic  10.2 us (5%)
    ppermute x5, starting transfers between devices, swap(): return lax.ppermute(value, axis, [(i, i ^ stride) for i in range(n)])  49.4 us
    ppermute x10, starting transfers between devices, side(): got[j] = lax.ppermute(sent[j], 'dp', SIDE)  40.7 us
    pallas_call x16, Pallas kernels, call(): pl.pallas_call(body, grid=(steps,), in_specs=in_specs, out_specs=out_spec...  37.2 us
    ppermute x10, waiting for transfers between devices, side(): got[j] = lax.ppermute(sent[j], 'dp', SIDE)  31.9 us
    unnamed x1, loops' own time  24.1 us
    ppermute x5, waiting for transfers between devices, swap(): return lax.ppermute(value, axis, [(i, i ^ stride) for i in range(n)])  19.3 us
    ppermute x8, starting transfers between devices, pipeline(): b[k] = lax.ppermute(q[k], 'dp', MID)  5.83 us
  transfers between devices with their start and end apart: 23, of which 15 were waited for; matrix products, arithmetic and copies ran while one was open for 1% of the time, Pallas kernels for 12%

commit v1 on v0

--- a/solution.py
+++ b/solution.py
@@ -273,9 +273,9 @@
     before = (jnp.arange(rows)[:, None] < jnp.arange(rows)[None, :]).astype(BF)
     rank = dot(hit.astype(BF), before)
     slots = experts * cap
-    sizes = sorted({slots * part // 16 for part in (6, 8, 16)}, reverse=True)
+    sizes = [slots, slots * 6 // 16, slots // 2]
     filled = jnp.sum(hit.astype(jnp.int32))
-    which = jnp.sum((filled <= jnp.array(sizes[1:], jnp.int32)).astype(jnp.int32))
+    which = jnp.where(filled <= sizes[1], 1, jnp.where(filled <= sizes[2], 2, 0))
     acted, gg, ug, mine, others = lax.switch(
         which,
         [functools.partial(pipeline, size, cap, scale) for size in sizes],

time: 226 us -> 217 us (0.960)
  loops' own time: 24.1 us -> 6.89 us
  other arithmetic: 10.2 us -> 17.6 us
  waiting for transfers between devices: 51.1 us -> 45.4 us
  starting transfers between devices: 95.9 us -> 99.4 us
  local copies, waits for them, and re-layouts: 1.32 us -> 4.14 us
    ppermute x5, starting transfers between devices: 49.4 us -> 4.78 us  [swap(): return lax.ppermute(value, axis, [(i, i ^ stride) for i in range(n)])]
    ppermute x10 -> x19, starting transfers between devices: 40.7 us -> 82.6 us  [side(): got[j] = lax.ppermute(sent[j], 'dp', SIDE)]
    unnamed x1, loops' own time: 24.1 us -> 6.89 us
    ppermute x10 -> x19, waiting for transfers between devices: 31.9 us -> 24.7 us  [side(): got[j] = lax.ppermute(sent[j], 'dp', SIDE)]
    ppermute x8 -> x16, starting transfers between devices: 5.83 us -> 12 us  [pipeline(): b[k] = lax.ppermute(q[k], 'dp', MID)]
    convert_element_type x10 -> x19, other arithmetic: 1.33 us -> 5.89 us  [add(): return (one.astype(F32) + two.astype(F32)).astype(HALF)]
    pallas_call x16 -> x32, Pallas kernels: 37.2 us -> 37.2 us  [call(): pl.pallas_call(body, grid=(steps,), in_specs=in_specs, out_specs=out_spec...]
  transfers between devices with their start and end apart: 23 -> 40, of which waited for: 15 -> 14; matrix products, arithmetic and copies ran while one was open for 1% -> 6% of each run, Pallas kernels for 12% -> 15%
where the time goes in v1:
time: 217 us; the launch traced here: 215 us
  starting transfers between devices  99.4 us (46%)
  waiting for transfers between devices  45.4 us (21%)
  Pallas kernels  37.2 us (17%)
  other arithmetic  17.6 us (8%)
  loops' own time  6.89 us (3%)
  local copies, waits for them, and re-layouts  4.14 us (2%)
  between operations  2.34 us (1%)
    ppermute x19, starting transfers between devices, side(): got[j] = lax.ppermute(sent[j], 'dp', SIDE)  82.6 us
    pallas_call x32, Pallas kernels, call(): pl.pallas_call(body, grid=(steps,), in_specs=in_specs, out_specs=out_spec...  37.2 us
    ppermute x19, waiting for transfers between devices, side(): got[j] = lax.ppermute(sent[j], 'dp', SIDE)  24.7 us
    ppermute x5, waiting for transfers between devices, swap(): return lax.ppermute(value, axis, [(i, i ^ stride) for i in range(n)])  20.7 us
    ppermute x16, starting transfers between devices, pipeline(): b[k] = lax.ppermute(q[k], 'dp', MID)  12 us
    unnamed x1, loops' own time  6.89 us
    convert_element_type x19, other arithmetic, add(): return (one.astype(F32) + two.astype(F32)).astype(HALF)  5.89 us
    ppermute x5, starting transfers between devices, swap(): return lax.ppermute(value, axis, [(i, i ^ stride) for i in range(n)])  4.78 us
  transfers between devices with their start and end apart: 40, of which 14 were waited for; matrix products, arithmetic and copies ran while one was open for 6% of the time, Pallas kernels for 15%

profile of v1, /device:TPU:0, one launch (start us, length us, event | category | flops | bytes accessed | tf_op | source)
XLA Modules:
  0.0 214.6 jit_solution(11381136256188648626)
XLA Ops:
  2.4 3.0 %collective-permute-start.71 = (bf16[128,896]{1,0:T(8,128)(2,1)S(1)}, bf16[128,896]{1,0:T(8,128)(2,1)S(1)}, u32[]{:S(2)}, u32[]{:S(2)}) collective-permute-start(bf16[128,896]{1,0:T(8,128)(2,1)S(1)} %fusion.56), channel_id=1, source_target_pairs={{0,8},{4,12},{8,0},{12,4},{1,9},{5,13},{9,1},{13,5},{2,10},{6,14},... | collective-permute-start | bytes 688136 | tf_op jit(solution)/shard_map/ppermute | solution.py:28
  5.4 5.6 %collective-permute-done.71 = bf16[128,896]{1,0:T(8,128)(2,1)S(1)} collective-permute-done((bf16[128,896]{1,0:T(8,128)(2,1)S(1)}, bf16[128,896]{1,0:T(8,128)(2,1)S(1)}, u32[]{:S(2)}, u32[]{:S(2)}) %collective-permute-start.71) | collective-permute-done | bytes 229408 | tf_op jit(solution)/shard_map/ppermute | solution.py:28
  16.5 181.9 %conditional.2 = (bf16[512,4096]{1,0:T(8,128)(2,1)}, bf16[768,4096]{1,0:T(8,128)(2,1)}, bf16[768,4096]{1,0:T(8,128)(2,1)}, bf16[256,768]{1,0:T(8,128)(2,1)S(1)}, f32[2,128,768]{2,1,0:T(8,128)S(1)}) conditional(s32[]{:T(128)} %clamp.3, (f32[4,128]{1,0:T(4,128)S(1)}, pred[4,128]{1,0:T(4,128)(4,1)S(1)}, bf16[512,768]{1,0:T(8,128)(2,1)S(1)}, ...), branch_computations={%region_2.3_spmd, %region_3.6_spmd, %region_6.9_spmd} | conditional | flops 873333760 | bytes 297162880
  26.6 3.3 %collective-permute-done = f16[512,512]{1,0:T(8,128)(2,1)} collective-permute-done((f16[512,512]{1,0:T(8,128)(2,1)}, f16[512,512]{1,0:T(8,128)(2,1)}, u32[]{:S(2)}, u32[]{:S(2)}) %collective-permute-start) | collective-permute-done | bytes 524320 | tf_op jit(solution)/shard_map/cond/branch_0_fun/ppermute | solution.py:233
  36.7 3.0 %collective-permute-done.1 = f16[512,512]{1,0:T(8,128)(2,1)} collective-permute-done((f16[512,512]{1,0:T(8,128)(2,1)S(1)}, f16[512,512]{1,0:T(8,128)(2,1)}, u32[]{:S(2)}, u32[]{:S(2)}) %collective-permute-start.1) | collective-permute-done | bytes 524320 | tf_op jit(solution)/shard_map/cond/branch_0_fun/ppermute | solution.py:233
  43.7 4.4 %collective-permute-start.7 = (f16[512,512]{1,0:T(8,128)(2,1)S(1)}, f16[512,512]{1,0:T(8,128)(2,1)S(1)}, u32[]{:S(2)}, u32[]{:S(2)}) collective-permute-start(f16[512,512]{1,0:T(8,128)(2,1)S(1)} %fusion.2), channel_id=1, source_target_pairs={{0,1},{1,0},{2,3},{3,2},{4,5},{5,4},{6,7},{7,6},{8,9},{9,8},{10,11... | collective-permute-start | bytes 1572872 | tf_op jit(solution)/shard_map/cond/branch_0_fun/ppermute | solution.py:233
  53.1 4.6 %collective-permute-start.5 = (f16[512,512]{1,0:T(8,128)(2,1)S(1)}, f16[512,512]{1,0:T(8,128)(2,1)S(1)}, u32[]{:S(2)}, u32[]{:S(2)}) collective-permute-start(f16[512,512]{1,0:T(8,128)(2,1)S(1)} %fusion.3), channel_id=1, source_target_pairs={{0,1},{1,0},{2,3},{3,2},{4,5},{5,4},{6,7},{7,6},{8,9},{9,8},{10,11... | collective-permute-start | bytes 1572872 | tf_op jit(solution)/shard_map/cond/branch_0_fun/ppermute | solution.py:233
  62.2 6.1 %collective-permute-start.9 = (f16[512,512]{1,0:T(8,128)(2,1)S(1)}, f16[512,512]{1,0:T(8,128)(2,1)S(1)}, u32[]{:S(2)}, u32[]{:S(2)}) collective-permute-start(f16[512,512]{1,0:T(8,128)(2,1)S(1)} %fusion.4), channel_id=1, source_target_pairs={{0,1},{1,0},{2,3},{3,2},{4,5},{5,4},{6,7},{7,6},{8,9},{9,8},{10,11... | collective-permute-start | bytes 1572872 | tf_op jit(solution)/shard_map/cond/branch_0_fun/ppermute | solution.py:233
  80.8 3.4 %collective-permute-start.13 = (f16[512,512]{1,0:T(8,128)(2,1)S(1)}, f16[512,512]{1,0:T(8,128)(2,1)S(1)}, u32[]{:S(2)}, u32[]{:S(2)}) collective-permute-start(f16[512,512]{1,0:T(8,128)(2,1)S(1)} %fusion.6), channel_id=1, source_target_pairs={{0,1},{1,0},{2,3},{3,2},{4,5},{5,4},{6,7},{7,6},{8,9},{9,8},{10,11... | collective-permute-start | bytes 1572872 | tf_op jit(solution)/shard_map/cond/branch_0_fun/ppermute | solution.py:233
  89.4 5.4 %collective-permute-start.17 = (f16[512,512]{1,0:T(8,128)(2,1)S(1)}, f16[512,512]{1,0:T(8,128)(2,1)S(1)}, u32[]{:S(2)}, u32[]{:S(2)}) collective-permute-start(f16[512,512]{1,0:T(8,128)(2,1)S(1)} %fusion.7), channel_id=1, source_target_pairs={{0,1},{1,0},{2,3},{3,2},{4,5},{5,4},{6,7},{7,6},{8,9},{9,8},{10,11... | collective-permute-start | bytes 1572872 | tf_op jit(solution)/shard_map/cond/branch_0_fun/ppermute | solution.py:233
  97.9 8.1 %collective-permute-start.15 = (f16[512,512]{1,0:T(8,128)(2,1)S(1)}, f16[512,512]{1,0:T(8,128)(2,1)S(1)}, u32[]{:S(2)}, u32[]{:S(2)}) collective-permute-start(f16[512,512]{1,0:T(8,128)(2,1)S(1)} %fusion.8), channel_id=1, source_target_pairs={{0,1},{1,0},{2,3},{3,2},{4,5},{5,4},{6,7},{7,6},{8,9},{9,8},{10,11... | collective-permute-start | bytes 1572872 | tf_op jit(solution)/shard_map/cond/branch_0_fun/ppermute | solution.py:233
  108.7 3.5 %collective-permute-start.19 = (f16[512,512]{1,0:T(8,128)(2,1)S(1)}, f16[512,512]{1,0:T(8,128)(2,1)S(1)}, u32[]{:S(2)}, u32[]{:S(2)}) collective-permute-start(f16[512,512]{1,0:T(8,128)(2,1)S(1)} %fusion.9), channel_id=1, source_target_pairs={{0,1},{1,0},{2,3},{3,2},{4,5},{5,4},{6,7},{7,6},{8,9},{9,8},{10,11... | collective-permute-start | bytes 1572872 | tf_op jit(solution)/shard_map/cond/branch_0_fun/ppermute | solution.py:233
  113.9 3.1 %collective-permute-done.15 = f16[512,512]{1,0:T(8,128)(2,1)S(1)} collective-permute-done((f16[512,512]{1,0:T(8,128)(2,1)S(1)}, f16[512,512]{1,0:T(8,128)(2,1)S(1)}, u32[]{:S(2)}, u32[]{:S(2)}) %collective-permute-start.15) | collective-permute-done | bytes 524320 | tf_op jit(solution)/shard_map/cond/branch_0_fun/ppermute | solution.py:233
  118.6 4.4 %collective-permute-start.23 = (f16[512,512]{1,0:T(8,128)(2,1)S(1)}, f16[512,512]{1,0:T(8,128)(2,1)S(1)}, u32[]{:S(2)}, u32[]{:S(2)}) collective-permute-start(f16[512,512]{1,0:T(8,128)(2,1)S(1)} %fusion.10), channel_id=1, source_target_pairs={{0,1},{1,0},{2,3},{3,2},{4,5},{5,4},{6,7},{7,6},{8,9},{9,8},{10,11... | collective-permute-start | bytes 1572872 | tf_op jit(solution)/shard_map/cond/branch_0_fun/ppermute | solution.py:233
  126.6 7.2 %collective-permute-start.21 = (f16[512,512]{1,0:T(8,128)(2,1)S(1)}, f16[512,512]{1,0:T(8,128)(2,1)S(1)}, u32[]{:S(2)}, u32[]{:S(2)}) collective-permute-start(f16[512,512]{1,0:T(8,128)(2,1)S(1)} %fusion.11), channel_id=1, source_target_pairs={{0,1},{1,0},{2,3},{3,2},{4,5},{5,4},{6,7},{7,6},{8,9},{9,8},{10,11... | collective-permute-start | bytes 1572872 | tf_op jit(solution)/shard_map/cond/branch_0_fun/ppermute | solution.py:233
  136.5 7.0 %collective-permute-start.25 = (f16[512,512]{1,0:T(8,128)(2,1)S(1)}, f16[512,512]{1,0:T(8,128)(2,1)S(1)}, u32[]{:S(2)}, u32[]{:S(2)}) collective-permute-start(f16[512,512]{1,0:T(8,128)(2,1)S(1)} %fusion.12), channel_id=1, source_target_pairs={{0,1},{1,0},{2,3},{3,2},{4,5},{5,4},{6,7},{7,6},{8,9},{9,8},{10,11... | collective-permute-start | bytes 1572872 | tf_op jit(solution)/shard_map/cond/branch_0_fun/ppermute | solution.py:233
  146.4 2.9 %collective-permute-start.29 = (f16[512,512]{1,0:T(8,128)(2,1)S(1)}, f16[512,512]{1,0:T(8,128)(2,1)S(1)}, u32[]{:S(2)}, u32[]{:S(2)}) collective-permute-start(f16[512,512]{1,0:T(8,128)(2,1)S(1)} %fusion.13), channel_id=1, source_target_pairs={{0,1},{1,0},{2,3},{3,2},{4,5},{5,4},{6,7},{7,6},{8,9},{9,8},{10,11... | collective-permute-start | bytes 1572872 | tf_op jit(solution)/shard_map/cond/branch_0_fun/ppermute | solution.py:233
  151.0 3.5 %collective-permute-done.25 = f16[512,512]{1,0:T(8,128)(2,1)S(1)} collective-permute-done((f16[512,512]{1,0:T(8,128)(2,1)S(1)}, f16[512,512]{1,0:T(8,128)(2,1)S(1)}, u32[]{:S(2)}, u32[]{:S(2)}) %collective-permute-start.25) | collective-permute-done | bytes 524320 | tf_op jit(solution)/shard_map/cond/branch_0_fun/ppermute | solution.py:233
  155.8 4.1 %collective-permute-start.27 = (f16[512,512]{1,0:T(8,128)(2,1)S(1)}, f16[512,512]{1,0:T(8,128)(2,1)S(1)}, u32[]{:S(2)}, u32[]{:S(2)}) collective-permute-start(f16[512,512]{1,0:T(8,128)(2,1)S(1)} %fusion.14), channel_id=1, source_target_pairs={{0,1},{1,0},{2,3},{3,2},{4,5},{5,4},{6,7},{7,6},{8,9},{9,8},{10,11... | collective-permute-start | bytes 1572872 | tf_op jit(solution)/shard_map/cond/branch_0_fun/ppermute | solution.py:233
  162.6 5.1 %collective-permute-start.32 = (f16[512,512]{1,0:T(8,128)(2,1)S(1)}, f16[512,512]{1,0:T(8,128)(2,1)S(1)}, u32[]{:S(2)}, u32[]{:S(2)}) collective-permute-start(f16[512,512]{1,0:T(8,128)(2,1)S(1)} %add_convert_fusion.3), channel_id=1, source_target_pairs={{0,1},{1,0},{2,3},{3,2},{4,5},{5,4},{6,7},{7,6},{8,9},{9,8},{10,11... | collective-permute-start | bytes 1572872 | tf_op jit(solution)/shard_map/cond/branch_0_fun/ppermute | solution.py:233
  175.2 5.7 %collective-permute-start.34 = (f16[512,512]{1,0:T(8,128)(2,1)S(1)}, f16[512,512]{1,0:T(8,128)(2,1)S(1)}, u32[]{:S(2)}, u32[]{:S(2)}) collective-permute-start(f16[512,512]{1,0:T(8,128)(2,1)S(1)} %add_convert_fusion), channel_id=1, source_target_pairs={{0,1},{1,0},{2,3},{3,2},{4,5},{5,4},{6,7},{7,6},{8,9},{9,8},{10,11... | collective-permute-start | bytes 1572872 | tf_op jit(solution)/shard_map/cond/branch_0_fun/ppermute | solution.py:233
  183.0 5.1 %collective-permute-done.34 = f16[512,512]{1,0:T(8,128)(2,1)S(1)} collective-permute-done((f16[512,512]{1,0:T(8,128)(2,1)S(1)}, f16[512,512]{1,0:T(8,128)(2,1)S(1)}, u32[]{:S(2)}, u32[]{:S(2)}) %collective-permute-start.34) | collective-permute-done | bytes 524320 | tf_op jit(solution)/shard_map/cond/branch_0_fun/ppermute | solution.py:233
  200.4 6.9 %collective-permute-done.74 = bf16[1,128,768]{2,1,0:T(8,128)(2,1)S(1)} collective-permute-done((bf16[1,128,768]{2,1,0:T(8,128)(2,1)S(1)}, bf16[1,128,768]{2,1,0:T(8,128)(2,1)S(1)}, u32[]{:S(2)}, u32[]{:S(2)}) %collective-permute-start.74) | collective-permute-done | bytes 196640 | tf_op jit(solution)/shard_map/ppermute | solution.py:28
  209.0 4.6 %collective-permute-done.75 = bf16[128,768]{1,0:T(8,128)(2,1)S(1)} collective-permute-done((bf16[128,768]{1,0:T(8,128)(2,1)S(1)}, bf16[128,768]{1,0:T(8,128)(2,1)S(1)}, u32[]{:S(2)}, u32[]{:S(2)}) %collective-permute-start.75) | collective-permute-done | bytes 196640 | tf_op jit(solution)/shard_map/ppermute | solution.py:28
  (193 shorter events, 95.3 us)
Async XLA Ops:
  23.0 16.8 %collective-permute-start.1 = (f16[512,512]{1,0:T(8,128)(2,1)S(1)}, f16[512,512]{1,0:T(8,128)(2,1)}, u32[]{:S(2)}, u32[]{:S(2)}) collective-permute-start(f16[512,512]{1,0:T(8,128)(2,1)S(1)} %multiply_convert_fusion.13), channel_id=1, source_target_pairs={{0,1},{1,0},{2,3},{3,2},{4,5},{5,4},{6,7},{7,6},{8,9},{9,8},{10,11... | collective-permute-start | bytes 1572872 | tf_op jit(solution)/shard_map/cond/branch_0_fun/ppermute | solution.py:233
  31.6 11.8 %collective-permute-start.4 = (f16[512,512]{1,0:T(8,128)(2,1)S(1)}, f16[512,512]{1,0:T(8,128)(2,1)S(1)}, u32[]{:S(2)}, u32[]{:S(2)}) collective-permute-start(f16[512,512]{1,0:T(8,128)(2,1)S(1)} %add_convert_fusion.31), channel_id=1, source_target_pairs={{1,2},{2,1},{5,6},{6,5},{9,10},{10,9},{13,14},{14,13},{17,18},{18,... | collective-permute-start | bytes 1572872 | tf_op jit(solution)/shard_map/cond/branch_0_fun/ppermute | solution.py:243
  39.7 12.2 %collective-permute-start.3 = (f16[512,512]{1,0:T(8,128)(2,1)S(1)}, f16[512,512]{1,0:T(8,128)(2,1)S(1)}, u32[]{:S(2)}, u32[]{:S(2)}) collective-permute-start(f16[512,512]{1,0:T(8,128)(2,1)S(1)} %multiply_convert_fusion.12), channel_id=1, source_target_pairs={{0,1},{1,0},{2,3},{3,2},{4,5},{5,4},{6,7},{7,6},{8,9},{9,8},{10,11... | collective-permute-start | bytes 1572872 | tf_op jit(solution)/shard_map/cond/branch_0_fun/ppermute | solution.py:233
  43.7 17.3 %collective-permute-start.7 = (f16[512,512]{1,0:T(8,128)(2,1)S(1)}, f16[512,512]{1,0:T(8,128)(2,1)S(1)}, u32[]{:S(2)}, u32[]{:S(2)}) collective-permute-start(f16[512,512]{1,0:T(8,128)(2,1)S(1)} %fusion.2), channel_id=1, source_target_pairs={{0,1},{1,0},{2,3},{3,2},{4,5},{5,4},{6,7},{7,6},{8,9},{9,8},{10,11... | collective-permute-start | bytes 1572872 | tf_op jit(solution)/shard_map/cond/branch_0_fun/ppermute | solution.py:233
  53.1 19.5 %collective-permute-start.5 = (f16[512,512]{1,0:T(8,128)(2,1)S(1)}, f16[512,512]{1,0:T(8,128)(2,1)S(1)}, u32[]{:S(2)}, u32[]{:S(2)}) collective-permute-start(f16[512,512]{1,0:T(8,128)(2,1)S(1)} %fusion.3), channel_id=1, source_target_pairs={{0,1},{1,0},{2,3},{3,2},{4,5},{5,4},{6,7},{7,6},{8,9},{9,8},{10,11... | collective-permute-start | bytes 1572872 | tf_op jit(solution)/shard_map/cond/branch_0_fun/ppermute | solution.py:233
  61.2 12.6 %collective-permute-start.10 = (f16[512,512]{1,0:T(8,128)(2,1)S(1)}, f16[512,512]{1,0:T(8,128)(2,1)S(1)}, u32[]{:S(2)}, u32[]{:S(2)}) collective-permute-start(f16[512,512]{1,0:T(8,128)(2,1)S(1)} %add_convert_fusion.26), channel_id=1, source_target_pairs={{1,2},{2,1},{5,6},{6,5},{9,10},{10,9},{13,14},{14,13},{17,18},{18,... | collective-permute-start | bytes 1572872 | tf_op jit(solution)/shard_map/cond/branch_0_fun/ppermute | solution.py:243
  62.2 17.5 %collective-permute-start.9 = (f16[512,512]{1,0:T(8,128)(2,1)S(1)}, f16[512,512]{1,0:T(8,128)(2,1)S(1)}, u32[]{:S(2)}, u32[]{:S(2)}) collective-permute-start(f16[512,512]{1,0:T(8,128)(2,1)S(1)} %fusion.4), channel_id=1, source_target_pairs={{0,1},{1,0},{2,3},{3,2},{4,5},{5,4},{6,7},{7,6},{8,9},{9,8},{10,11... | collective-permute-start | bytes 1572872 | tf_op jit(solution)/shard_map/cond/branch_0_fun/ppermute | solution.py:233
  74.1 14.1 %collective-permute-start.11 = (f16[512,512]{1,0:T(8,128)(2,1)S(1)}, f16[512,512]{1,0:T(8,128)(2,1)S(1)}, u32[]{:S(2)}, u32[]{:S(2)}) collective-permute-start(f16[512,512]{1,0:T(8,128)(2,1)S(1)} %fusion.5), channel_id=1, source_target_pairs={{0,1},{1,0},{2,3},{3,2},{4,5},{5,4},{6,7},{7,6},{8,9},{9,8},{10,11... | collective-permute-start | bytes 1572872 | tf_op jit(solution)/shard_map/cond/branch_0_fun/ppermute | solution.py:233
  80.8 15.8 %collective-permute-start.13 = (f16[512,512]{1,0:T(8,128)(2,1)S(1)}, f16[512,512]{1,0:T(8,128)(2,1)S(1)}, u32[]{:S(2)}, u32[]{:S(2)}) collective-permute-start(f16[512,512]{1,0:T(8,128)(2,1)S(1)} %fusion.6), channel_id=1, source_target_pairs={{0,1},{1,0},{2,3},{3,2},{4,5},{5,4},{6,7},{7,6},{8,9},{9,8},{10,11... | collective-permute-start | bytes 1572872 | tf_op jit(solution)/shard_map/cond/branch_0_fun/ppermute | solution.py:233
  89.4 18.1 %collective-permute-start.17 = (f16[512,512]{1,0:T(8,128)(2,1)S(1)}, f16[512,512]{1,0:T(8,128)(2,1)S(1)}, u32[]{:S(2)}, u32[]{:S(2)}) collective-permute-start(f16[512,512]{1,0:T(8,128)(2,1)S(1)} %fusion.7), channel_id=1, source_target_pairs={{0,1},{1,0},{2,3},{3,2},{4,5},{5,4},{6,7},{7,6},{8,9},{9,8},{10,11... | collective-permute-start | bytes 1572872 | tf_op jit(solution)/shard_map/cond/branch_0_fun/ppermute | solution.py:233
  96.7 11.7 %collective-permute-start.16 = (f16[512,512]{1,0:T(8,128)(2,1)S(1)}, f16[512,512]{1,0:T(8,128)(2,1)S(1)}, u32[]{:S(2)}, u32[]{:S(2)}) collective-permute-start(f16[512,512]{1,0:T(8,128)(2,1)S(1)} %add_convert_fusion.18), channel_id=1, source_target_pairs={{1,2},{2,1},{5,6},{6,5},{9,10},{10,9},{13,14},{14,13},{17,18},{18,... | collective-permute-start | bytes 1572872 | tf_op jit(solution)/shard_map/cond/branch_0_fun/ppermute | solution.py:243
  97.9 19.2 %collective-permute-start.15 = (f16[512,512]{1,0:T(8,128)(2,1)S(1)}, f16[512,512]{1,0:T(8,128)(2,1)S(1)}, u32[]{:S(2)}, u32[]{:S(2)}) collective-permute-start(f16[512,512]{1,0:T(8,128)(2,1)S(1)} %fusion.8), channel_id=1, source_target_pairs={{0,1},{1,0},{2,3},{3,2},{4,5},{5,4},{6,7},{7,6},{8,9},{9,8},{10,11... | collective-permute-start | bytes 1572872 | tf_op jit(solution)/shard_map/cond/branch_0_fun/ppermute | solution.py:233
  107.7 10.6 %collective-permute-start.20 = (f16[512,512]{1,0:T(8,128)(2,1)S(1)}, f16[512,512]{1,0:T(8,128)(2,1)S(1)}, u32[]{:S(2)}, u32[]{:S(2)}) collective-permute-start(f16[512,512]{1,0:T(8,128)(2,1)S(1)} %add_convert_fusion.16), channel_id=1, source_target_pairs={{1,2},{2,1},{5,6},{6,5},{9,10},{10,9},{13,14},{14,13},{17,18},{18,... | collective-permute-start | bytes 1572872 | tf_op jit(solution)/shard_map/cond/branch_0_fun/ppermute | solution.py:243
  108.7 16.6 %collective-permute-start.19 = (f16[512,512]{1,0:T(8,128)(2,1)S(1)}, f16[512,512]{1,0:T(8,128)(2,1)S(1)}, u32[]{:S(2)}, u32[]{:S(2)}) collective-permute-start(f16[512,512]{1,0:T(8,128)(2,1)S(1)} %fusion.9), channel_id=1, source_target_pairs={{0,1},{1,0},{2,3},{3,2},{4,5},{5,4},{6,7},{7,6},{8,9},{9,8},{10,11... | collective-permute-start | bytes 1572872 | tf_op jit(solution)/shard_map/cond/branch_0_fun/ppermute | solution.py:233
  118.6 16.8 %collective-permute-start.23 = (f16[512,512]{1,0:T(8,128)(2,1)S(1)}, f16[512,512]{1,0:T(8,128)(2,1)S(1)}, u32[]{:S(2)}, u32[]{:S(2)}) collective-permute-start(f16[512,512]{1,0:T(8,128)(2,1)S(1)} %fusion.10), channel_id=1, source_target_pairs={{0,1},{1,0},{2,3},{3,2},{4,5},{5,4},{6,7},{7,6},{8,9},{9,8},{10,11... | collective-permute-start | bytes 1572872 | tf_op jit(solution)/shard_map/cond/branch_0_fun/ppermute | solution.py:233
  125.5 10.8 %collective-permute-start.22 = (f16[512,512]{1,0:T(8,128)(2,1)S(1)}, f16[512,512]{1,0:T(8,128)(2,1)S(1)}, u32[]{:S(2)}, u32[]{:S(2)}) collective-permute-start(f16[512,512]{1,0:T(8,128)(2,1)S(1)} %add_convert_fusion.12), channel_id=1, source_target_pairs={{1,2},{2,1},{5,6},{6,5},{9,10},{10,9},{13,14},{14,13},{17,18},{18,... | collective-permute-start | bytes 1572872 | tf_op jit(solution)/shard_map/cond/branch_0_fun/ppermute | solution.py:243
  126.6 18.6 %collective-permute-start.21 = (f16[512,512]{1,0:T(8,128)(2,1)S(1)}, f16[512,512]{1,0:T(8,128)(2,1)S(1)}, u32[]{:S(2)}, u32[]{:S(2)}) collective-permute-start(f16[512,512]{1,0:T(8,128)(2,1)S(1)} %fusion.11), channel_id=1, source_target_pairs={{0,1},{1,0},{2,3},{3,2},{4,5},{5,4},{6,7},{7,6},{8,9},{9,8},{10,11... | collective-permute-start | bytes 1572872 | tf_op jit(solution)/shard_map/cond/branch_0_fun/ppermute | solution.py:233
  135.6 10.6 %collective-permute-start.26 = (f16[512,512]{1,0:T(8,128)(2,1)S(1)}, f16[512,512]{1,0:T(8,128)(2,1)S(1)}, u32[]{:S(2)}, u32[]{:S(2)}) collective-permute-start(f16[512,512]{1,0:T(8,128)(2,1)S(1)} %add_convert_fusion.10), channel_id=1, source_target_pairs={{1,2},{2,1},{5,6},{6,5},{9,10},{10,9},{13,14},{14,13},{17,18},{18,... | collective-permute-start | bytes 1572872 | tf_op jit(solution)/shard_map/cond/branch_0_fun/ppermute | solution.py:243
  136.5 17.9 %collective-permute-start.25 = (f16[512,512]{1,0:T(8,128)(2,1)S(1)}, f16[512,512]{1,0:T(8,128)(2,1)S(1)}, u32[]{:S(2)}, u32[]{:S(2)}) collective-permute-start(f16[512,512]{1,0:T(8,128)(2,1)S(1)} %fusion.12), channel_id=1, source_target_pairs={{0,1},{1,0},{2,3},{3,2},{4,5},{5,4},{6,7},{7,6},{8,9},{9,8},{10,11... | collective-permute-start | bytes 1572872 | tf_op jit(solution)/shard_map/cond/branch_0_fun/ppermute | solution.py:233
  146.4 15.1 %collective-permute-start.29 = (f16[512,512]{1,0:T(8,128)(2,1)S(1)}, f16[512,512]{1,0:T(8,128)(2,1)S(1)}, u32[]{:S(2)}, u32[]{:S(2)}) collective-permute-start(f16[512,512]{1,0:T(8,128)(2,1)S(1)} %fusion.13), channel_id=1, source_target_pairs={{0,1},{1,0},{2,3},{3,2},{4,5},{5,4},{6,7},{7,6},{8,9},{9,8},{10,11... | collective-permute-start | bytes 1572872 | tf_op jit(solution)/shard_map/cond/branch_0_fun/ppermute | solution.py:233
  155.8 13.7 %collective-permute-start.27 = (f16[512,512]{1,0:T(8,128)(2,1)S(1)}, f16[512,512]{1,0:T(8,128)(2,1)S(1)}, u32[]{:S(2)}, u32[]{:S(2)}) collective-permute-start(f16[512,512]{1,0:T(8,128)(2,1)S(1)} %fusion.14), channel_id=1, source_target_pairs={{0,1},{1,0},{2,3},{3,2},{4,5},{5,4},{6,7},{7,6},{8,9},{9,8},{10,11... | collective-permute-start | bytes 1572872 | tf_op jit(solution)/shard_map/cond/branch_0_fun/ppermute | solution.py:233
  162.6 18.6 %collective-permute-start.32 = (f16[512,512]{1,0:T(8,128)(2,1)S(1)}, f16[512,512]{1,0:T(8,128)(2,1)S(1)}, u32[]{:S(2)}, u32[]{:S(2)}) collective-permute-start(f16[512,512]{1,0:T(8,128)(2,1)S(1)} %add_convert_fusion.3), channel_id=1, source_target_pairs={{0,1},{1,0},{2,3},{3,2},{4,5},{5,4},{6,7},{7,6},{8,9},{9,8},{10,11... | collective-permute-start | bytes 1572872 | tf_op jit(solution)/shard_map/cond/branch_0_fun/ppermute | solution.py:233
  170.7 12.3 %collective-permute-start.33 = (f16[512,512]{1,0:T(8,128)(2,1)S(1)}, f16[512,512]{1,0:T(8,128)(2,1)S(1)}, u32[]{:S(2)}, u32[]{:S(2)}) collective-permute-start(f16[512,512]{1,0:T(8,128)(2,1)S(1)} %add_convert_fusion.1), channel_id=1, source_target_pairs={{0,1},{1,0},{2,3},{3,2},{4,5},{5,4},{6,7},{7,6},{8,9},{9,8},{10,11... | collective-permute-start | bytes 1572872 | tf_op jit(solution)/shard_map/cond/branch_0_fun/ppermute | solution.py:233
  175.2 12.9 %collective-permute-start.34 = (f16[512,512]{1,0:T(8,128)(2,1)S(1)}, f16[512,512]{1,0:T(8,128)(2,1)S(1)}, u32[]{:S(2)}, u32[]{:S(2)}) collective-permute-start(f16[512,512]{1,0:T(8,128)(2,1)S(1)} %add_convert_fusion), channel_id=1, source_target_pairs={{0,1},{1,0},{2,3},{3,2},{4,5},{5,4},{6,7},{7,6},{8,9},{9,8},{10,11... | collective-permute-start | bytes 1572872 | tf_op jit(solution)/shard_map/cond/branch_0_fun/ppermute | solution.py:233
  (29 other events, 175.8 us)
